TPU v7x, 512 devices: a whole 4x4x16 slice. The times are simulated.
512 devices in a mesh: fsdp: 32 (over z_lo, x, core), replica: 16 (over z_hi, y).
Axes of the slice: x: 4, y: 4, z: 16 (z_hi: 4, z_lo: 4; z = z_hi * 4 + z_lo), core: 2. Of those that a mesh axis runs over, the one named last changes fastest.
Arguments:
- master: float32 [1792, 128, 128], P('fsdp', 'replica'), may hold values from -0.0625 to 0.0625
- gradient: bfloat16 [1792, 128, 128], P('fsdp', 'replica'), may hold values from -6 to 6
- first_moment: float32 [1792, 128, 128], P('fsdp', 'replica'), may hold values from -4 to 4
- second_moment: float32 [1792, 128, 128], P('fsdp', 'replica'), may hold values from 0.05 to 2
- owner_counts: int32 [32], replicated, may hold values from 1 to 84, 1792 in all
Outputs:
- master_new: float32 [1792, 128, 128], P('fsdp', 'replica')
- first_new: float32 [1792, 128, 128], P('fsdp', 'replica')
- second_new: float32 [1792, 128, 128], P('fsdp', 'replica')
- rollout_codes: bfloat16 [2688, 128, 128], P('fsdp')
- rollout_scales: bfloat16 [2688], P('fsdp')
Inputs may be any that keep to these rules, and one draw needn't show every extreme that they name: owner_counts sum to 1792; the largest is exactly 84.
All inputs are finite; a program needn't handle non-finite values.
Results may differ from a plain program's by a relative error of at most 0.014.
Values may be sent and summed in bfloat16 or wider, within the bound.
A program may use at most 64 MiB of HBM per device.

v0:
```python
import jax
import jax.numpy as jnp
from jax import lax
from jax.sharding import PartitionSpec as P

EXPERTS = 2
RB = 16
CB = 56


RATE = 0.003
BETA_ONE = 0.9
BETA_TWO = 0.95
EPSILON = 1e-08
DECAY = 0.1
CORRECT_ONE = 0.99997343861
CORRECT_TWO = 0.99407947


def rollout_index_of(learner_ids):
    expert_of = learner_ids // (RB * CB)
    within = learner_ids % (RB * CB)
    row_block = within // CB
    col_block = within % CB
    return expert_of * (RB * CB) + col_block * RB + row_block


def learner_index_of(position):
    expert_of = position // (RB * CB)
    within = position % (RB * CB)
    col_block = within // RB
    row_block = within % RB
    return expert_of * (RB * CB) + row_block * CB + col_block


def on_device(master, gradient, first_moment, second_moment, owner_counts):
    tile_count, row_count, col_count = master.shape
    holders = lax.axis_size("fsdp")
    holder_index = lax.axis_index("fsdp")
    grad_float = gradient.astype(jnp.float32)
    first_new = BETA_ONE * first_moment + (1.0 - BETA_ONE) * grad_float
    second_new = BETA_TWO * second_moment + (1.0 - BETA_TWO) * grad_float * grad_float
    direction = first_new / CORRECT_ONE / (jnp.sqrt(second_new / CORRECT_TWO) + EPSILON)
    master_new = master - RATE * (direction + DECAY * master)
    local_peak = jnp.max(jnp.abs(master_new), axis=(1, 2))
    block_peak = lax.pmax(local_peak, "replica")
    scales = (block_peak + 1e-06).astype(jnp.bfloat16)
    code_tiles = (master_new / scales.astype(jnp.float32)[:, None, None]).astype(jnp.bfloat16)
    all_tiles = EXPERTS * RB * CB
    cap_own = all_tiles * 3 // (2 * holders)
    cap_send = min(tile_count, tile_count // CB * (cap_own // RB + 2))
    range_end = jnp.cumsum(owner_counts)
    range_start = range_end - owner_counts
    learner_ids = holder_index * tile_count + jnp.arange(tile_count, dtype=jnp.int32)
    rollout_ids = rollout_index_of(learner_ids)
    target = jnp.sum((rollout_ids[:, None] >= range_end[None, :]).astype(jnp.int32), axis=1)
    earlier = (target[:, None] == target[None, :]) & (rollout_ids[None, :] < rollout_ids[:, None])
    slot_index = jnp.sum(earlier.astype(jnp.int32), axis=1)
    destination = target * cap_send + slot_index
    send_codes = (
        jnp.zeros((holders * cap_send, row_count, col_count), jnp.bfloat16)
        .at[destination]
        .set(code_tiles)
    )
    send_scales = jnp.zeros((holders * cap_send,), jnp.bfloat16).at[destination].set(scales)
    got_codes, got_scales = (
        lax.all_to_all(send_codes, "fsdp", split_axis=0, concat_axis=0, tiled=True),
        lax.all_to_all(send_scales, "fsdp", split_axis=0, concat_axis=0, tiled=True),
    )
    holder_start = range_start[holder_index]
    holder_total = owner_counts[holder_index]
    position = jnp.arange(cap_own, dtype=jnp.int32)
    filled = position < holder_total
    wanted = jnp.where(filled, holder_start + position, 0)
    source_ids = learner_index_of(wanted)
    sender = source_ids // tile_count
    same_sender = (sender[:, None] == sender[None, :]) & (position[None, :] < position[:, None])
    slot_back = jnp.sum(same_sender.astype(jnp.int32), axis=1)
    pick = jnp.where(filled, sender * cap_send + slot_back, 0)
    zero_code = jnp.zeros((), jnp.bfloat16)
    filled_tile = filled[:, None, None]
    picked = jnp.where(filled_tile, got_codes[pick], zero_code)
    rollout_codes = lax.all_gather(picked, "replica", axis=1, tiled=True)
    rollout_scales = jnp.where(filled, got_scales[pick], zero_code)
    return (master_new, first_new, second_new, rollout_codes, rollout_scales)


def solution(mesh):
    return jax.shard_map(
        on_device,
        mesh=mesh,
        in_specs=(
            P("fsdp", "replica", None),
            P("fsdp", "replica", None),
            P("fsdp", "replica", None),
            P("fsdp", "replica", None),
            P(),
        ),
        out_specs=(
            P("fsdp", "replica", None),
            P("fsdp", "replica", None),
            P("fsdp", "replica", None),
            P("fsdp", None, None),
            P("fsdp"),
        ),
        check_vma=False,
    )
```

profile of v0, /device:TPU:2, one launch (start us, length us, event | category | flops | bytes accessed | tf_op | source)
XLA Modules:
  0.0 216.7 jit_solution(15005335064663282087)
XLA Ops:
  7.2 0.8 copy.14
  8.0 0.1 reduce
  8.2 0.2 convert_reduce_fusion.1
  8.4 2.3 %abs_reduce_fusion = (f32[56]{0:T(128)S(1)}, f32[56,8,128]{2,1,0:T(8,128)S(1)}, f32[56,8,128]{2,1,0:T(8,128)}, f32[56,8,128]{2,1,0:T(8,128)}) fusion(f32[56,8,128]{2,1,0:T(8,128)} %param.5, bf16[56,8,128]{2,1,0:T(8,128)(2,1)} %param.6, f32[56,8,128]{2,1,0:T(8,128)} %param.7, f32[56,8,128]{2,1,0:T(8,128)} %param.8), kind=kLoop, calls=%fused_computation.9 | loop fusion | flops 1032136 | bytes 1491168 | tf_op jit(solution)/shard_map/reduce_max | solution.py:45
  10.7 59.5 %pmax.7 = f32[56]{0:T(128)S(1)} all-reduce(f32[56]{0:T(128)S(1)} %get-tuple-element.5), channel_id=1, replica_groups=mesh['fsdp'=32,'replica'=16] {'replica'}, use_global_device_ids=true, to_apply=%region_4.5 | all-reduce | flops 56 | bytes 448 | tf_op jit(solution)/shard_map/pmax | solution.py:46
  70.2 0.1 divide_convert_fusion
  70.4 0.8 broadcast_in_dim.27
  71.2 6.9 %scatter_fusion = bf16[224,8,128]{2,1,0:T(8,128)(2,1)} fusion(bf16[224,8,128]{2,1,0:T(8,128)(2,1)} %broadcast_in_dim.27, s32[56]{0:T(128)S(1)} %fusion.12, bf16[56,8,128]{2,1,0:T(8,128)(2,1)S(1)} %divide_convert_fusion), kind=kCustom, calls=%fused_computation.2 | custom fusion | bytes 344288 | tf_op jit(solution)/shard_map/scatter | solution.py:63
  78.2 6.4 %all-to-all-start = ((bf16[224,8,128]{2,1,0:T(8,128)(2,1)}), bf16[224,8,128]{2,1,0:T(8,128)(2,1)S(1)}, u32[]{:S(2)}, u32[]{:S(2)}) async-start(bf16[224,8,128]{2,1,0:T(8,128)(2,1)} %scatter_fusion), calls=%async_computation | async-start | bytes 917504 | tf_op jit(solution)/shard_map/all_to_all | solution.py:67
  84.6 0.7 dynamic_slice.6
  85.2 0.6 dynamic_slice.7
  85.8 0.7 iota_compare_fusion.1
  86.5 1.4 and_select_fusion
  87.9 0.2 convert_reduce_fusion
  88.0 1.4 fusion.13
  89.4 8.4 %all-to-all-done = bf16[224,8,128]{2,1,0:T(8,128)(2,1)S(1)} async-done(((bf16[224,8,128]{2,1,0:T(8,128)(2,1)}), bf16[224,8,128]{2,1,0:T(8,128)(2,1)S(1)}, u32[]{:S(2)}, u32[]{:S(2)}) %all-to-all-start) | async-done | bytes 458784 | tf_op jit(solution)/shard_map/all_to_all | solution.py:67
  97.8 0.6 gather_fusion
  98.5 0.8 broadcast_select_fusion
  99.3 0.9 scatter_custom_fusion.1
  100.3 12.2 %all_to_all.18 = bf16[32,7,1]{1,2,0:T(2,128)(2,1)S(1)} all-to-all(bf16[32,7,1]{1,2,0:T(2,128)(2,1)S(1)} %all_to_all.15), channel_id=1, replica_groups=mesh['fsdp'=32,'replica'=16] {'fsdp'}, dimensions={0} | all-to-all | bytes 896 | tf_op jit(solution)/shard_map/all_to_all | solution.py:68
  112.7 1.2 gather_fusion.1
  113.9 1.2 broadcast_select_fusion.1
  115.1 91.1 %all-gather.2.cloned.1.call-done = bf16[84,128,128]{2,1,0:T(8,128)(2,1)} async-done(((bf16[84,8,128]{2,1,0:T(8,128)(2,1)}), bf16[84,128,128]{2,1,0:T(8,128)(2,1)}) %all-gather.2.cloned.1.call-update) | async-done | bytes 2752528 | tf_op jit(solution)/shard_map/all_gather | solution.py:83
  206.2 3.7 %copy.18 = bf16[84,128,128]{2,1,0:T(8,128)(2,1)} copy(bf16[84,128,128]{2,1,0:T(8,128)(2,1)} %all-gather.2.cloned.1.call-done) | data formatting | bytes 5505024
  (16 shorter events, 0.6 us)
Async XLA Ops:
  7.2 77.4 %copy-start.1 = (s32[32]{0:T(128)S(1)}, s32[32]{0:T(128)}, u32[]{:S(2)}) copy-start(s32[32]{0:T(128)} %param.9) | copy-start | bytes 388
  10.7 199.1 %copy-start = (f32[56,8,128]{2,1,0:T(8,128)}, f32[56,8,128]{2,1,0:T(8,128)S(1)}, u32[]{:S(2)}) copy-start(f32[56,8,128]{2,1,0:T(8,128)S(1)} %get-tuple-element.16) | copy-start | bytes 688132
  78.2 19.7 %all-to-all-start = ((bf16[224,8,128]{2,1,0:T(8,128)(2,1)}), bf16[224,8,128]{2,1,0:T(8,128)(2,1)S(1)}, u32[]{:S(2)}, u32[]{:S(2)}) async-start(bf16[224,8,128]{2,1,0:T(8,128)(2,1)} %scatter_fusion), calls=%async_computation | async-start | bytes 917504 | tf_op jit(solution)/shard_map/all_to_all | solution.py:67
  84.5 121.7 %all-gather.2.cloned.1.call-start = ((), (), s32[]{:S(2)}) async-start(), calls=%async_computation.2 | async-start | bytes 2924544 | tf_op jit(solution)/shard_map/all_gather | solution.py:83
Sparse Core Ops, SparseCore 0:
  99.4 106.7 all-gather.1
where the time goes:
time: 217 us
  waiting for transfers between devices  99.5 us (46%)
  blocking collectives  71.7 us (33%)
  local copies, waits for them, and re-layouts  16.5 us (8%)
  between operations  14.1 us (6%)
  other arithmetic  8.58 us (4%)
  starting transfers between devices  6.39 us (3%)
    all_gather x1, waiting for transfers between devices, on_device(): rollout_codes = lax.all_gather(picked, 'replica', axis=1, tiled=True)  91.1 us
    pmax x1, blocking collectives, on_device(): block_peak = lax.pmax(local_peak, 'replica')  59.5 us
    all_to_all x1, blocking collectives, on_device(): lax.all_to_all(send_scales, 'fsdp', split_axis=0, concat_axis=0, tiled=True)  12.2 us
    all_to_all x1, waiting for transfers between devices, on_device(): lax.all_to_all(send_codes, 'fsdp', split_axis=0, concat_axis=0, tiled=True)  8.38 us
    scatter x1, local copies, waits for them, and re-layouts, on_device(): send_codes = jnp.zeros((holders * cap_send, row_count, col_count), jnp.bf...  6.95 us
    all_to_all x1, starting transfers between devices, on_device(): lax.all_to_all(send_codes, 'fsdp', split_axis=0, concat_axis=0, tiled=True)  6.35 us
  transfers between devices with their start and end apart: 2, of which 2 were waited for; matrix products, arithmetic and copies ran while one was open for 4% of the time, Pallas kernels for 0%

commit v1 on v0

v1 whole, which is shorter than its diff:
```python
import functools

import jax
import jax.numpy as jnp
from jax import lax
from jax.experimental import pallas as pl
from jax.experimental.pallas import tpu as pltpu
from jax.sharding import PartitionSpec as P

MESH = pl.DeviceIdType.MESH

RB = 16
CB = 56
CAP_OWN = 84
HOLDERS = 32
COPIES = 16

RATE = 0.003
BETA_ONE = 0.9
BETA_TWO = 0.95
EPSILON = 1e-08
DECAY = 0.1
CORRECT_ONE = 0.99997343861
CORRECT_TWO = 0.99407947

ROWS = 8
LANES = 128
PER_PAIR = 6
OWN_ROWS = CAP_OWN * ROWS
PIECES = ((0, 256), (256, 256), (512, 160))
ALIKE = 32 * ROWS


def adam(master, gradient, first_moment, second_moment):
    grad_float = gradient.astype(jnp.float32)
    first_new = BETA_ONE * first_moment + (1.0 - BETA_ONE) * grad_float
    second_new = BETA_TWO * second_moment + (1.0 - BETA_TWO) * grad_float * grad_float
    direction = first_new / CORRECT_ONE / (jnp.sqrt(second_new / CORRECT_TWO) + EPSILON)
    master_new = master - RATE * (direction + DECAY * master)
    return master_new, first_new, second_new


def prepare(
    counts_ref, master_ref, gradient_ref, first_ref, second_ref,
    master_out, first_out, second_out, send, peak, place_ref,
    starts, raw,
):
    f = lax.axis_index("fsdp")
    e, r = f // RB, lax.rem(f, RB)

    pad = PER_PAIR * ROWS
    raw[pl.ds(0, pad), :] = jnp.zeros((pad, LANES), jnp.float32)
    raw[pl.ds(pad + CB * ROWS, pad), :] = jnp.zeros((pad, LANES), jnp.float32)
    lane = lax.broadcasted_iota(jnp.int32, (ROWS, LANES), 1)
    row = lax.broadcasted_iota(jnp.int32, (ROWS, LANES), 0)
    span = 8 * ROWS

    def update(step, peaks):
        here = pl.ds(pl.multiple_of(step * span, span), span)
        master_new, first_new, second_new = adam(
            master_ref[here, :], gradient_ref[here, :], first_ref[here, :], second_ref[here, :]
        )
        master_out[here, :] = master_new
        first_out[here, :] = first_new
        second_out[here, :] = second_new
        raw[pl.ds(pl.multiple_of(pad + step * span, 16), span), :] = master_new
        tall = jnp.max(jnp.abs(master_new).reshape(8, ROWS, LANES), axis=1)
        return jnp.where(lane == row + step * 8, jnp.max(tall, axis=1, keepdims=True), peaks)

    peaks = lax.fori_loop(0, CB // 8, update, jnp.zeros((ROWS, LANES), jnp.float32))
    peak[...] = jnp.broadcast_to(jnp.max(peaks, axis=0, keepdims=True), (ROWS, LANES))

    def total(o, start):
        starts[o] = start
        return start + counts_ref[o]

    lax.fori_loop(0, HOLDERS, total, 0)

    def pack(step, carry):
        first = ((starts[lax.rem(f + step, HOLDERS)] - r + (RB - 1)) >> 4) - CB * e
        first = jnp.clip(first, -PER_PAIR, CB) + PER_PAIR
        here = pl.ds(pl.multiple_of(first * ROWS, ROWS), PER_PAIR * ROWS)
        send[pl.ds(pl.multiple_of(step * 48, 16), 48), :] = raw[here, :].astype(jnp.bfloat16)
        return carry

    lax.fori_loop(0, HOLDERS, pack, 0)
    place_ref[pl.ds(0, 8), :] = jnp.full((ROWS, LANES), starts[f], jnp.int32)
    place_ref[pl.ds(8, 8), :] = jnp.full((ROWS, LANES), counts_ref[f], jnp.int32)


def exchange(
    send, first_peak, place_ref,
    all_ref, inverse_ref, scales_ref,
    recv, own, peak, peak_z, peak_y, table,
    a2a_send, a2a_recv, peak_send, peak_recv, gather_send, z_near, z_far, y_near, y_far, local_sem,
):
    f = lax.axis_index("fsdp")
    rep = lax.axis_index("replica")
    zh, y = rep // 4, lax.rem(rep, 4)

    def at_z(step):
        return {"replica": lax.rem(zh + step + 4, 4) * 4 + y}

    def at_y(step):
        return {"replica": zh * 4 + lax.rem(y + step + 4, 4)}

    def at_f(step):
        return {"fsdp": lax.rem(f + step, HOLDERS)}

    barrier = pltpu.get_barrier_semaphore()

    def greet(step, carry):
        pl.semaphore_signal(barrier, inc=1, device_id=at_f(step), device_id_type=MESH)
        return carry

    lax.fori_loop(1, HOLDERS, greet, 0)
    for step in (1, 2, 3):
        pl.semaphore_signal(barrier, inc=1, device_id=at_z(step), device_id_type=MESH)
        pl.semaphore_signal(barrier, inc=1, device_id=at_y(step), device_id_type=MESH)

    for piece in range(3):
        recv[pl.ds(piece * 512, 16), :] = send[pl.ds(piece * 16, 16), :]
    peak[...] = first_peak[...]
    lane = lax.broadcasted_iota(jnp.int32, (ROWS, LANES), 1)
    row = lax.broadcasted_iota(jnp.int32, (ROWS, LANES), 0)
    start = place_ref[pl.ds(0, 8), :]
    count = place_ref[pl.ds(8, 8), :]
    odd = [(start & (1 << bit)) != 0 for bit in range(4)]

    pl.semaphore_wait(barrier, HOLDERS - 1 + 6)

    for piece in range(3):

        def give(step, carry, piece=piece):
            pltpu.make_async_remote_copy(
                src_ref=send.at[pl.ds(pl.multiple_of(step * 48 + piece * 16, 16), 16)],
                dst_ref=recv.at[pl.ds(pl.multiple_of(piece * 512 + step * 16, 16), 16)],
                send_sem=a2a_send,
                recv_sem=a2a_recv.at[piece],
                device_id=at_f(step),
                device_id_type=MESH,
            ).start()
            return carry

        lax.fori_loop(1, HOLDERS, give, 0)

    def tell(source, target, send_sem, recv_sem, device):
        copy = pltpu.make_async_remote_copy(
            src_ref=source, dst_ref=target, send_sem=send_sem, recv_sem=recv_sem, device_id=device, device_id_type=MESH
        )
        copy.start()

    def landed(target, sem):
        pltpu.make_async_copy(target, target, sem).wait()

    for step in (1, 2, 3):
        tell(peak, peak_z.at[pl.ds((step - 1) * 8, 8)], peak_send.at[0], peak_recv.at[0], at_z(step))

    def order(piece):
        halves = [[], []]
        for r in range(RB):
            found = []
            for e in range(2):
                away = lax.rem(f - (e * RB + r) + HOLDERS, HOLDERS)
                pair = recv[pl.ds(pl.multiple_of(piece * 512 + away * 16, 16), 16), :]
                found.append(pair.astype(jnp.float32))
            position = start + ((r - start) & (RB - 1)) + piece * 32
            for half in range(2):
                here = slice(half * 8, half * 8 + 8)
                late = position >= RB * CB - half * 16
                halves[half].append(jnp.where(late, found[1][here, :], found[0][here, :]))
        for half in range(2):
            tiles = halves[half]
            for bit in range(4):
                tiles = [jnp.where(odd[bit], tiles[(k + (1 << bit)) % RB], tiles[k]) for k in range(RB)]
            slots = min(RB, PIECES[piece][1] // ROWS - half * RB)
            for k in range(0, slots, 2):
                both = jnp.concatenate([tiles[k], tiles[k + 1]], axis=0).astype(jnp.bfloat16)
                own[pl.ds((piece * 32 + half * 16 + k) * ROWS, 16), :] = both

    def chunk(z, yy, low, number):
        place = (z * 4 + yy) * OWN_ROWS + low
        return all_ref.at[pl.ds(pl.multiple_of(place, 16), number)]

    def z_at(step):
        return lax.rem(zh + step + 4, 4)

    def y_at(step):
        return lax.rem(y + step + 4, 4)

    def send_y(z_step, piece):
        low, number = PIECES[piece]
        place = chunk(z_at(z_step), y, low, number)
        source = own.at[pl.ds(low, number)] if z_step == 0 else place
        for way, step in enumerate((1, -1)):
            tell(source, place, gather_send, y_near.at[way, z_step, piece], at_y(step))

    locals_ = []
    for piece, (low, number) in enumerate(PIECES):
        landed(recv.at[pl.ds(piece * 512 + 16, 31 * 16)], a2a_recv.at[piece])
        order(piece)
        here = own.at[pl.ds(low, number)]
        for way, step in enumerate((1, -1)):
            tell(here, chunk(zh, y, low, number), gather_send, z_near.at[way, piece], at_z(step))
        send_y(0, piece)
        keep = pltpu.make_async_copy(here, chunk(zh, y, low, number), local_sem.at[piece])
        keep.start()
        locals_.append(keep)

    def relay_z(piece):
        low, number = PIECES[piece]
        part = number // 2
        for way, step in enumerate((1, -1)):
            landed(chunk(z_at(-step), y, low, number), z_near.at[way, piece])
            half = chunk(z_at(-step), y, low + way * part, part)
            tell(half, half, gather_send, z_far.at[way, piece], at_z(step))
            send_y((-step) % 4, piece)

    def finish_z(piece):
        low, number = PIECES[piece]
        part = number // 2
        for way in range(2):
            landed(chunk(z_at(2), y, low + way * part, part), z_far.at[way, piece])
        send_y(2, piece)

    def relay_y(z_step, piece):
        low, number = PIECES[piece]
        part = number // 2
        for way, step in enumerate((1, -1)):
            landed(chunk(z_at(z_step), y_at(-step), low, number), y_near.at[way, z_step, piece])
            half = chunk(z_at(z_step), y_at(-step), low + way * part, part)
            tell(half, half, gather_send, y_far.at[way, z_step, piece], at_y(step))

    def peaks_y():
        landed(peak_z, peak_recv.at[0])
        landed(peak_z, peak_send.at[0])
        best = peak[...]
        for step in range(3):
            best = jnp.maximum(best, peak_z[pl.ds(step * 8, 8), :])
        peak[...] = best
        for step in (1, 2, 3):
            tell(peak, peak_y.at[pl.ds((step - 1) * 8, 8)], peak_send.at[1], peak_recv.at[1], at_y(step))

    def peaks_f():
        landed(peak_y, peak_recv.at[1])
        landed(peak_y, peak_send.at[1])
        best = peak[...]
        for step in range(3):
            best = jnp.maximum(best, peak_y[pl.ds(step * 8, 8), :])
        table[pl.ds(0, 8), :] = best

        def spread(step, carry):
            tell(
                table.at[pl.ds(0, 8)],
                table.at[pl.ds(pl.multiple_of(step * 8, 8), 8)],
                peak_send.at[2],
                peak_recv.at[2],
                at_f(step),
            )
            return carry

        lax.fori_loop(1, HOLDERS, spread, 0)

    def scales():
        others = table.at[pl.ds(8, 31 * 8)]
        landed(others, peak_recv.at[2])
        landed(others, peak_send.at[2])

        flat = jnp.zeros((ROWS, LANES), jnp.float32)
        for step in range(11):
            slot = step * 8 + row
            u = start + slot
            late = u >= RB * CB
            away = (f - (u & (RB - 1)) - jnp.where(late, RB, 0)) & (HOLDERS - 1)
            found = jnp.zeros((ROWS, LANES), jnp.float32)
            for source in range(HOLDERS):
                found = jnp.where(away == source, table[pl.ds(source * 8, 8), :], found)
            column = (u >> 4) - jnp.where(late, CB, 0)
            top = jnp.max(jnp.where(lane == column, found, 0.0), axis=1, keepdims=True)
            scale = jnp.broadcast_to((top + 1e-06).astype(jnp.bfloat16).astype(jnp.float32), (ROWS, LANES))
            filled = slot < count
            inverse_ref[pl.ds(step * 8, 8), :] = jnp.where(filled, 1.0 / scale, 0.0)
            flat = jnp.where((lane == slot) & filled, scale, flat)
        scales_ref[...] = jnp.broadcast_to(jnp.max(flat, axis=0, keepdims=True), (ROWS, LANES))

    relay_y(0, 0)
    relay_z(0)
    peaks_y()
    relay_y(0, 1)
    relay_z(1)
    relay_y(0, 2)
    peaks_f()
    relay_y(1, 0)
    relay_y(3, 0)
    finish_z(0)
    relay_z(2)
    relay_y(1, 1)
    relay_y(3, 1)
    finish_z(1)
    scales()
    relay_y(2, 0)
    finish_z(2)
    relay_y(1, 2)
    relay_y(3, 2)
    relay_y(2, 1)
    relay_y(2, 2)
    for piece, (low, number) in enumerate(PIECES):
        part = number // 2
        for z_step in range(4):
            for way in range(2):
                landed(chunk(z_at(z_step), y_at(2), low + way * part, part), y_far.at[way, z_step, piece])
    for keep in locals_:
        keep.wait()
    landed(send.at[pl.ds(48, 31 * 48)], a2a_send)
    landed(all_ref.at[pl.ds(0, 15 * OWN_ROWS)], gather_send)


def finish(all_ref, inverse_ref, codes_ref):
    inverse = inverse_ref[...][:, None, :]
    for pair in range(COPIES // 2):
        parts = [all_ref[2 * pair + i].astype(jnp.float32).reshape(8, ROWS, LANES) for i in range(2)]
        both = jnp.concatenate(parts, axis=1)
        codes = jnp.where(inverse > 0.0, both * inverse, 0.0)
        codes_ref[:, pl.ds(pair * 16, 16), :] = codes.astype(jnp.bfloat16)


def on_device(master, gradient, first_moment, second_moment, owner_counts):
    tiles, rows, lanes = master.shape
    flat = [a.reshape(tiles * rows, lanes) for a in (master, gradient, first_moment, second_moment)]
    vmem = pl.BlockSpec(memory_space=pltpu.VMEM)
    dma = pltpu.SemaphoreType.DMA
    part = jax.ShapeDtypeStruct((tiles * rows, lanes), jnp.float32)
    tile = jax.ShapeDtypeStruct((ROWS, LANES), jnp.float32)
    master_new, first_new, second_new, send, peak, place = pl.pallas_call(
        prepare,
        out_shape=(
            part, part, part,
            jax.ShapeDtypeStruct((HOLDERS * 48, LANES), jnp.bfloat16),
            tile,
            jax.ShapeDtypeStruct((2 * ROWS, LANES), jnp.int32),
        ),
        in_specs=[pl.BlockSpec(memory_space=pltpu.SMEM)] + [vmem] * 4,
        out_specs=(vmem,) * 6,
        scratch_shapes=[
            pltpu.SMEM((HOLDERS,), jnp.int32),
            pltpu.VMEM(((CB + 2 * PER_PAIR) * ROWS, LANES), jnp.float32),
        ],
        name="prepare",
    )(owner_counts, *flat)
    gathered, inverse, scales = pl.pallas_call(
        exchange,
        out_shape=(
            jax.ShapeDtypeStruct((COPIES * OWN_ROWS, LANES), jnp.bfloat16),
            jax.ShapeDtypeStruct((88, LANES), jnp.float32),
            tile,
        ),
        in_specs=[vmem] * 3,
        out_specs=(vmem, vmem, vmem),
        scratch_shapes=[
            pltpu.VMEM((3 * 512, LANES), jnp.bfloat16),
            pltpu.VMEM((OWN_ROWS, LANES), jnp.bfloat16),
            pltpu.VMEM((ROWS, LANES), jnp.float32),
            pltpu.VMEM((3 * ROWS, LANES), jnp.float32),
            pltpu.VMEM((3 * ROWS, LANES), jnp.float32),
            pltpu.VMEM((HOLDERS * ROWS, LANES), jnp.float32),
            dma,
            dma((3,)),
            dma((3,)),
            dma((3,)),
            dma,
            dma((2, 3)),
            dma((2, 3)),
            dma((2, 4, 3)),
            dma((2, 4, 3)),
            dma((3,)),
        ],
        compiler_params=pltpu.CompilerParams(collective_id=0, has_side_effects=True, vmem_limit_bytes=40 << 20),
        name="exchange",
    )(send, peak, place)
    codes = pl.pallas_call(
        finish,
        grid=(11,),
        out_shape=jax.ShapeDtypeStruct((CAP_OWN, 128, 128), jnp.bfloat16),
        in_specs=[
            pl.BlockSpec((COPIES, 8 * ROWS, LANES), lambda i: (0, i, 0)),
            pl.BlockSpec((8, LANES), lambda i: (i, 0)),
        ],
        out_specs=pl.BlockSpec((8, 128, 128), lambda i: (i, 0, 0)),
        compiler_params=pltpu.CompilerParams(vmem_limit_bytes=40 << 20),
        name="finish",
    )(gathered.reshape(COPIES, OWN_ROWS, LANES), inverse)
    shape = (tiles, rows, lanes)
    rollout_scales = scales[0, :CAP_OWN].astype(jnp.bfloat16)
    return master_new.reshape(shape), first_new.reshape(shape), second_new.reshape(shape), codes, rollout_scales


def solution(mesh):
    split = P("fsdp", "replica", None)
    return jax.shard_map(
        on_device,
        mesh=mesh,
        in_specs=(split, split, split, split, P()),
        out_specs=(split, split, split, P("fsdp", None, None), P("fsdp")),
        check_vma=False,
    )
```

time: 217 us -> 75.2 us (0.35)
  the two profiles are of different devices: /device:TPU:2 before, /device:TPU:68 now
where the time goes in v1:
time: 75.2 us; the launch traced here: 74.9 us
  Pallas kernels  71.4 us (95%)
  local copies, waits for them, and re-layouts  2.89 us (4%)
    pallas_call x1, Pallas kernels, on_device(): pl.pallas_call(exchange, out_shape=(jax.ShapeDtypeStruct((COPIES * OWN_RO...  62.7 us
    pallas_call x1, Pallas kernels, on_device(): pl.pallas_call(finish, grid=(11,), out_shape=jax.ShapeDtypeStruct((CAP_OW...  4.99 us
    pallas_call x1, Pallas kernels, on_device(): pl.pallas_call(prepare, out_shape=(part, part, part, jax.ShapeDtypeStruct...  3.65 us
    unnamed x6, local copies, waits for them, and re-layouts  2.38 us

profile of v1, /device:TPU:68, one launch (start us, length us, event | category | flops | bytes accessed | tf_op | source)
XLA Modules:
  0.0 74.9 jit_solution(11442546282397731762)
XLA Ops:
  0.6 3.6 %prepare.1 = (f32[448,128]{1,0:T(8,128)}, f32[448,128]{1,0:T(8,128)}, f32[448,128]{1,0:T(8,128)}, bf16[1536,128]{1,0:T(8,128)(2,1)}, f32[8,128]{1,0:T(8,128)}, /*index=5*/s32[16,128]{1,0:T(8,128)}) custom-call(s32[32]{0:T(128)} %counts_ref.1, f32[448,128]{1,0:T(8,128)} %bitcast.11, bf16[448,128]{1,0:T(8,128)(2,1)} %bitcast.14, f32[448,128]{1,0:T(8,128)} %bitcast.12, ...), custom_call_target="tpu_custom_call" | custom-call | tf_op jit(solution)/shard_map/prepare/pallas_call | solution.py:334
  4.3 0.0 copy-start
  4.3 1.0 %copy-done = bf16[1536,128]{1,0:T(8,128)(2,1)S(1)} copy-done((bf16[1536,128]{1,0:T(8,128)(2,1)S(1)}, bf16[1536,128]{1,0:T(8,128)(2,1)}, u32[]{:S(2)}) %copy-start) | copy-done | bytes 393240
  5.3 0.0 copy-start.1
  5.3 0.7 copy-done.1
  6.0 0.0 copy-start.2
  6.0 0.7 copy-done.2
  6.7 62.7 %exchange.1 = (bf16[10752,128]{1,0:T(8,128)(2,1)S(1)}, f32[88,128]{1,0:T(8,128)S(1)}, f32[8,128]{1,0:T(8,128)S(1)}) custom-call(bf16[1536,128]{1,0:T(8,128)(2,1)S(1)} %copy-done, f32[8,128]{1,0:T(8,128)S(1)} %copy-done.2, s32[16,128]{1,0:T(8,128)S(1)} %copy-done.1), custom_call_target="tpu_custom_call" | custom-call | tf_op jit(solution)/shard_map/exchange/pallas_call | solution.py:350
  69.4 5.0 %finish.1 = bf16[84,128,128]{2,1,0:T(8,128)(2,1)} custom-call(bf16[16,672,128]{2,1,0:T(8,128)(2,1)S(1)} %bitcast.10, f32[88,128]{1,0:T(8,128)S(1)} %get-tuple-element.21.inverse_ref), custom_call_target="tpu_custom_call" | custom-call | tf_op jit(solution)/shard_map/finish/pallas_call | solution.py:380
  74.4 0.5 slice_bitcast_fusion
  (1 shorter events, 0.0 us)
Async XLA Ops:
  4.3 1.0 %copy-start = (bf16[1536,128]{1,0:T(8,128)(2,1)S(1)}, bf16[1536,128]{1,0:T(8,128)(2,1)}, u32[]{:S(2)}) copy-start(bf16[1536,128]{1,0:T(8,128)(2,1)} %get-tuple-element.17.send) | copy-start | bytes 1179652
  5.3 0.7 copy-start.1
  6.0 0.7 copy-start.2

commit v2 on v1

v2 whole, which is shorter than its diff:
```python
import functools

import jax
import jax.numpy as jnp
from jax import lax
from jax.experimental import pallas as pl
from jax.experimental.pallas import tpu as pltpu
from jax.sharding import PartitionSpec as P

MESH = pl.DeviceIdType.MESH

RB = 16
CB = 56
CAP_OWN = 84
HOLDERS = 32
COPIES = 16

RATE = 0.003
BETA_ONE = 0.9
BETA_TWO = 0.95
EPSILON = 1e-08
DECAY = 0.1
CORRECT_ONE = 0.99997343861
CORRECT_TWO = 0.99407947

ROWS = 8
LANES = 128
PER_PAIR = 6
OWN_ROWS = CAP_OWN * ROWS
PIECES = ((0, 256), (256, 256), (512, 160))
VMEM_LIMIT = 63 << 20
GROUP = 16
REACH = 22


def adam(master, gradient, first_moment, second_moment):
    grad_float = gradient.astype(jnp.float32)
    first_new = BETA_ONE * first_moment + (1.0 - BETA_ONE) * grad_float
    second_new = BETA_TWO * second_moment + (1.0 - BETA_TWO) * grad_float * grad_float
    direction = first_new / CORRECT_ONE / (jnp.sqrt(second_new / CORRECT_TWO) + EPSILON)
    master_new = master - RATE * (direction + DECAY * master)
    return master_new, first_new, second_new


def exchange(
    counts_ref, master_in, gradient_in, first_in, second_in,
    all_ref, inverse_ref, scales_ref,
    master_ref, gradient_ref, first_ref, second_ref, in_sem, raw, send, recv, own, peak, peak_z, peak_y, table,
    a2a_send, a2a_recv, peak_send, peak_recv, gather_send, z_near, z_far, y_near, y_far, local_sem,
):
    f = lax.axis_index("fsdp")
    rep = lax.axis_index("replica")
    zh, y = rep // 4, lax.rem(rep, 4)
    e, r = f // RB, lax.rem(f, RB)
    lowest = e * (HOLDERS - REACH)
    wide = (f >= HOLDERS - REACH) & (f < REACH)

    def at_z(step):
        return {"replica": lax.rem(zh + step + 4, 4) * 4 + y}

    def at_y(step):
        return {"replica": zh * 4 + lax.rem(y + step + 4, 4)}

    def at_f(step):
        return {"fsdp": lax.rem(f + step, HOLDERS)}

    inputs = ((master_in, master_ref), (gradient_in, gradient_ref), (first_in, first_ref), (second_in, second_ref))
    inputs = [pltpu.make_async_copy(source, target, in_sem.at[i]) for i, (source, target) in enumerate(inputs)]
    for copy in inputs:
        copy.start()
    barrier = pltpu.get_barrier_semaphore()

    def greet(step, carry):
        source = lax.rem(f + step, HOLDERS)

        @pl.when(((source < RB) & (f < REACH)) | ((source >= RB) & (f >= HOLDERS - REACH)))
        def _():
            pl.semaphore_signal(barrier, inc=1, device_id={"fsdp": source}, device_id_type=MESH)

        return carry

    lax.fori_loop(1, HOLDERS, greet, 0)
    for step in (1, 2, 3):
        pl.semaphore_signal(barrier, inc=1, device_id=at_z(step), device_id_type=MESH)
        pl.semaphore_signal(barrier, inc=1, device_id=at_y(step), device_id_type=MESH)

    lane = lax.broadcasted_iota(jnp.int32, (ROWS, LANES), 1)
    row = lax.broadcasted_iota(jnp.int32, (ROWS, LANES), 0)
    for copy in inputs:
        copy.wait()
    span = 8 * ROWS
    peaks = jnp.zeros((ROWS, LANES), jnp.float32)
    for step in range(CB // 8):
        here = pl.ds(step * span, span)
        master_new, _, _ = adam(master_ref[here, :], gradient_ref[here, :], first_ref[here, :], second_ref[here, :])
        raw[here, :] = master_new.astype(jnp.bfloat16)
        tall = jnp.max(jnp.abs(master_new).reshape(8, ROWS, LANES), axis=1)
        peaks = jnp.where(lane == row + step * 8, jnp.max(tall, axis=1, keepdims=True), peaks)
    peak[...] = jnp.broadcast_to(jnp.max(peaks, axis=0, keepdims=True), (ROWS, LANES))

    begins = [jnp.int32(0)]
    for o in range(HOLDERS - 1):
        begins.append(begins[-1] + counts_ref[o])
    line = lax.broadcasted_iota(jnp.int32, (48, LANES), 0)
    column = lax.broadcasted_iota(jnp.int32, (48, LANES), 1)
    for i in range(REACH):
        begin = begins[i] + e * (begins[i + HOLDERS - REACH] - begins[i])
        first = ((jnp.full((48, LANES), begin, jnp.int32) - r + (RB - 1)) >> 4) - CB * e
        place = first * ROWS + line - column
        packed = jnp.zeros((48, LANES), jnp.float32)
        for low in range(0, CB * ROWS, LANES):
            width = min(LANES, CB * ROWS - low)
            ones = jnp.where(place == low, 1.0, 0.0).astype(jnp.bfloat16)[:, :width]
            packed += jnp.dot(ones, raw[pl.ds(low, width), :], preferred_element_type=jnp.float32)
        send[pl.ds(i * 48, 48), :] = packed.astype(jnp.bfloat16)
    for piece in range(3):
        mine = send[pl.ds(pl.multiple_of((f - lowest) * 48 + piece * 16, 16), 16), :]
        recv[pl.ds(pl.multiple_of(piece * 512 + f * 16, 16), 16), :] = mine

    begin = begins[HOLDERS - 1] * 0
    for o in range(1, HOLDERS):
        begin += jnp.where(f == o, 1, 0) * begins[o]
    start = jnp.full((ROWS, LANES), begin, jnp.int32)
    count = jnp.full((ROWS, LANES), counts_ref[f], jnp.int32)
    odd = [(start & (1 << bit)) != 0 for bit in range(4)]

    pl.semaphore_wait(barrier, REACH - 1 + 6)

    def owners(give):
        def visit(step, carry):
            i = lax.rem(f + step, REACH)

            @pl.when(lowest + i != f)
            def _():
                give(i)

            return carry

        lax.fori_loop(0, REACH, visit, 0)

    for piece in range(3):

        def give(i, piece=piece):
            pltpu.make_async_remote_copy(
                src_ref=send.at[pl.ds(pl.multiple_of(i * 48 + piece * 16, 16), 16)],
                dst_ref=recv.at[pl.ds(pl.multiple_of(piece * 512 + f * 16, 16), 16)],
                send_sem=a2a_send,
                recv_sem=a2a_recv.at[piece],
                device_id={"fsdp": lowest + i},
                device_id_type=MESH,
            ).start()

        owners(give)

    def tell(source, target, send_sem, recv_sem, device):
        copy = pltpu.make_async_remote_copy(
            src_ref=source, dst_ref=target, send_sem=send_sem, recv_sem=recv_sem, device_id=device, device_id_type=MESH
        )
        copy.start()

    def landed(target, sem):
        pltpu.make_async_copy(target, target, sem).wait()

    def landed_from_all(buffer, low, rows, sem):
        @pl.when(wide)
        def _():
            landed(buffer.at[pl.ds(low, (HOLDERS - 1) * rows)], sem)

        @pl.when(jnp.logical_not(wide))
        def _():
            landed(buffer.at[pl.ds(low, (RB - 1) * rows)], sem)

    for step in (1, 2, 3):
        tell(peak, peak_z.at[pl.ds((step - 1) * 8, 8)], peak_send.at[0], peak_recv.at[0], at_z(step))

    def order(piece):
        halves = [[], []]
        for r in range(RB):
            found = []
            for e in range(2):
                pair = recv[pl.ds(piece * 512 + (e * RB + r) * 16, 16), :]
                found.append(pair.astype(jnp.float32))
            position = start + ((r - start) & (RB - 1)) + piece * 32
            for half in range(2):
                here = slice(half * 8, half * 8 + 8)
                late = position >= RB * CB - half * 16
                halves[half].append(jnp.where(late, found[1][here, :], found[0][here, :]))
        for half in range(2):
            tiles = halves[half]
            for bit in range(4):
                tiles = [jnp.where(odd[bit], tiles[(k + (1 << bit)) % RB], tiles[k]) for k in range(RB)]
            slots = min(RB, PIECES[piece][1] // ROWS - half * RB)
            for k in range(0, slots, 2):
                both = jnp.concatenate([tiles[k], tiles[k + 1]], axis=0).astype(jnp.bfloat16)
                own[pl.ds((piece * 32 + half * 16 + k) * ROWS, 16), :] = both

    def chunk(z, yy, low, number):
        place = (z * 4 + yy) * OWN_ROWS + low
        return all_ref.at[pl.ds(pl.multiple_of(place, 16), number)]

    def z_at(step):
        return lax.rem(zh + step + 4, 4)

    def y_at(step):
        return lax.rem(y + step + 4, 4)

    def send_y(z_step, piece):
        low, number = PIECES[piece]
        place = chunk(z_at(z_step), y, low, number)
        source = own.at[pl.ds(low, number)] if z_step == 0 else place
        for way, step in enumerate((1, -1)):
            tell(source, place, gather_send, y_near.at[way, z_step, piece], at_y(step))

    locals_ = []
    for piece, (low, number) in enumerate(PIECES):
        landed_from_all(recv, piece * 512, 16, a2a_recv.at[piece])
        order(piece)
        here = own.at[pl.ds(low, number)]
        for way, step in enumerate((1, -1)):
            tell(here, chunk(zh, y, low, number), gather_send, z_near.at[way, piece], at_z(step))
        send_y(0, piece)
        keep = pltpu.make_async_copy(here, chunk(zh, y, low, number), local_sem.at[piece])
        keep.start()
        locals_.append(keep)

    def relay_z(piece):
        low, number = PIECES[piece]
        part = number // 2
        for way, step in enumerate((1, -1)):
            landed(chunk(z_at(-step), y, low, number), z_near.at[way, piece])
            half = chunk(z_at(-step), y, low + way * part, part)
            tell(half, half, gather_send, z_far.at[way, piece], at_z(step))
            send_y((-step) % 4, piece)

    def finish_z(piece):
        low, number = PIECES[piece]
        part = number // 2
        for way in range(2):
            landed(chunk(z_at(2), y, low + way * part, part), z_far.at[way, piece])
        send_y(2, piece)

    def relay_y(z_step, piece):
        low, number = PIECES[piece]
        part = number // 2
        for way, step in enumerate((1, -1)):
            landed(chunk(z_at(z_step), y_at(-step), low, number), y_near.at[way, z_step, piece])
            half = chunk(z_at(z_step), y_at(-step), low + way * part, part)
            tell(half, half, gather_send, y_far.at[way, z_step, piece], at_y(step))

    def peaks_y():
        landed(peak_z, peak_recv.at[0])
        landed(peak_z, peak_send.at[0])
        best = peak[...]
        for step in range(3):
            best = jnp.maximum(best, peak_z[pl.ds(step * 8, 8), :])
        peak[...] = best
        for step in (1, 2, 3):
            tell(peak, peak_y.at[pl.ds((step - 1) * 8, 8)], peak_send.at[1], peak_recv.at[1], at_y(step))

    def peaks_f():
        landed(peak_y, peak_recv.at[1])
        landed(peak_y, peak_send.at[1])
        best = peak[...]
        for step in range(3):
            best = jnp.maximum(best, peak_y[pl.ds(step * 8, 8), :])
        mine = table.at[pl.ds(pl.multiple_of(f * 8, 8), 8)]
        mine[...] = best

        def give(i):
            tell(mine, mine, peak_send.at[2], peak_recv.at[2], {"fsdp": lowest + i})

        owners(give)

    def scales():
        landed_from_all(table, 0, 8, peak_recv.at[2])
        landed(table.at[pl.ds(0, (REACH - 1) * 8)], peak_send.at[2])

        flat = jnp.zeros((ROWS, LANES), jnp.float32)
        for step in range(11):
            slot = step * 8 + row
            u = start + slot
            late = u >= RB * CB
            origin = (u & (RB - 1)) + jnp.where(late, RB, 0)
            found = jnp.zeros((ROWS, LANES), jnp.float32)
            for source in range(HOLDERS):
                found = jnp.where(origin == source, table[pl.ds(source * 8, 8), :], found)
            column = (u >> 4) - jnp.where(late, CB, 0)
            top = jnp.max(jnp.where(lane == column, found, 0.0), axis=1, keepdims=True)
            scale = jnp.broadcast_to((top + 1e-06).astype(jnp.bfloat16).astype(jnp.float32), (ROWS, LANES))
            filled = slot < count
            inverse_ref[pl.ds(step * 8, 8), :] = jnp.where(filled, 1.0 / scale, 0.0)
            flat = jnp.where((lane == slot) & filled, scale, flat)
        scales_ref[...] = jnp.broadcast_to(jnp.max(flat, axis=0, keepdims=True), (ROWS, LANES))

    relay_y(0, 0)
    relay_z(0)
    peaks_y()
    relay_y(0, 1)
    relay_z(1)
    relay_y(0, 2)
    peaks_f()
    relay_y(1, 0)
    relay_y(3, 0)
    finish_z(0)
    relay_z(2)
    relay_y(1, 1)
    relay_y(3, 1)
    finish_z(1)
    scales()
    relay_y(2, 0)
    finish_z(2)
    relay_y(1, 2)
    relay_y(3, 2)
    relay_y(2, 1)
    relay_y(2, 2)
    for piece, (low, number) in enumerate(PIECES):
        part = number // 2
        for z_step in range(4):
            for way in range(2):
                landed(chunk(z_at(z_step), y_at(2), low + way * part, part), y_far.at[way, z_step, piece])
    for keep in locals_:
        keep.wait()
    landed(send.at[pl.ds(0, (REACH - 1) * 48)], a2a_send)
    landed(all_ref.at[pl.ds(0, 15 * OWN_ROWS)], gather_send)


def finish(
    all_ref, inverse_ref, scale_ref, master_ref, gradient_ref, first_ref, second_ref,
    codes_ref, scales_ref, master_out, first_out, second_out,
    tiles, codes, inverse, master, gradient, first, second, master_to, first_to, second_to,
    tile_sem, small_sem, out_sem,
):
    def started(source, target, sem):
        copy = pltpu.make_async_copy(source, target, sem)
        copy.start()
        return copy

    small = [
        started(source, target, small_sem.at[i])
        for i, (source, target) in enumerate(
            ((master_ref, master), (gradient_ref, gradient), (first_ref, first), (second_ref, second), (inverse_ref, inverse))
        )
    ]
    steps = [(low, min(GROUP, CAP_OWN - low)) for low in range(0, CAP_OWN, GROUP)]
    arriving = []
    for i, (low, slots) in enumerate(steps):
        rows = pl.ds(low * ROWS, slots * ROWS)
        arriving.append(started(all_ref.at[:, rows, :], tiles.at[:, rows, :], tile_sem.at[i]))
    for copy in small:
        copy.wait()
    leaving = []
    span = 8 * ROWS

    def update(step, carry):
        here = pl.ds(pl.multiple_of(step * span, span), span)
        master_new, first_new, second_new = adam(master[here, :], gradient[here, :], first[here, :], second[here, :])
        master_to[here, :] = master_new
        first_to[here, :] = first_new
        second_to[here, :] = second_new
        return carry

    lax.fori_loop(0, CB // 8, update, 0)
    for i, (source, target) in enumerate(((master_to, master_out), (first_to, first_out), (second_to, second_out))):
        leaving.append(started(source, target, out_sem.at[i]))
    for i, (low, slots) in enumerate(steps):
        arriving[i].wait()
        for base in range(low, low + slots, 8):
            number = min(8, CAP_OWN - base)
            factor = inverse[pl.ds(base, number), :][:, None, :]
            for pair in range(COPIES // 2):
                parts = [
                    tiles[2 * pair + k, pl.ds(base * ROWS, number * ROWS), :].astype(jnp.float32).reshape(number, ROWS, LANES)
                    for k in range(2)
                ]
                both = jnp.concatenate(parts, axis=1)
                coded = jnp.where(factor > 0.0, both * factor, 0.0).astype(jnp.bfloat16)
                codes[pl.ds(base, number), pl.ds(pair * 16, 16), :] = coded
        here = pl.ds(low, slots)
        leaving.append(started(codes.at[here], codes_ref.at[here], out_sem.at[3 + i]))
    scales_ref[...] = scale_ref[0, :][:CAP_OWN].astype(jnp.bfloat16)
    for copy in leaving:
        copy.wait()


def on_device(master, gradient, first_moment, second_moment, owner_counts):
    tiles, rows, lanes = master.shape
    flat = [a.reshape(tiles * rows, lanes) for a in (master, gradient, first_moment, second_moment)]
    vmem = pl.BlockSpec(memory_space=pltpu.VMEM)
    hbm = pl.BlockSpec(memory_space=pl.ANY)
    dma = pltpu.SemaphoreType.DMA
    part = jax.ShapeDtypeStruct((tiles * rows, lanes), jnp.float32)
    tile = jax.ShapeDtypeStruct((ROWS, LANES), jnp.float32)
    own = pltpu.VMEM((tiles * rows, lanes), jnp.float32)
    gathered, inverse, scales = pl.pallas_call(
        exchange,
        out_shape=(
            jax.ShapeDtypeStruct((COPIES * OWN_ROWS, LANES), jnp.bfloat16),
            jax.ShapeDtypeStruct((88, LANES), jnp.float32),
            tile,
        ),
        in_specs=[pl.BlockSpec(memory_space=pltpu.SMEM)] + [hbm] * 4,
        out_specs=(vmem, vmem, vmem),
        scratch_shapes=[
            own, pltpu.VMEM((tiles * rows, lanes), jnp.bfloat16), own, own,
            dma((4,)),
            pltpu.VMEM((CB * ROWS, LANES), jnp.bfloat16),
            pltpu.VMEM((REACH * 48, LANES), jnp.bfloat16),
            pltpu.VMEM((3 * 512, LANES), jnp.bfloat16),
            pltpu.VMEM((OWN_ROWS, LANES), jnp.bfloat16),
            pltpu.VMEM((ROWS, LANES), jnp.float32),
            pltpu.VMEM((3 * ROWS, LANES), jnp.float32),
            pltpu.VMEM((3 * ROWS, LANES), jnp.float32),
            pltpu.VMEM((HOLDERS * ROWS, LANES), jnp.float32),
            dma,
            dma((3,)),
            dma((3,)),
            dma((3,)),
            dma,
            dma((2, 3)),
            dma((2, 3)),
            dma((2, 4, 3)),
            dma((2, 4, 3)),
            dma((3,)),
        ],
        compiler_params=pltpu.CompilerParams(collective_id=0, has_side_effects=True, vmem_limit_bytes=VMEM_LIMIT),
        name="exchange",
    )(owner_counts, *flat)
    steps = -(-CAP_OWN // GROUP)
    codes, rollout_scales, master_new, first_new, second_new = pl.pallas_call(
        finish,
        out_shape=(
            jax.ShapeDtypeStruct((CAP_OWN, 128, 128), jnp.bfloat16),
            jax.ShapeDtypeStruct((CAP_OWN,), jnp.bfloat16),
            part, part, part,
        ),
        in_specs=[hbm, hbm, vmem] + [hbm] * 4,
        out_specs=(hbm, vmem, hbm, hbm, hbm),
        scratch_shapes=[
            pltpu.VMEM((COPIES, OWN_ROWS, LANES), jnp.bfloat16),
            pltpu.VMEM((CAP_OWN, 128, 128), jnp.bfloat16),
            pltpu.VMEM((88, LANES), jnp.float32),
            own, pltpu.VMEM((tiles * rows, lanes), jnp.bfloat16), own, own, own, own, own,
            dma((steps,)),
            dma((5,)),
            dma((3 + steps,)),
        ],
        compiler_params=pltpu.CompilerParams(vmem_limit_bytes=VMEM_LIMIT),
        name="finish",
    )(gathered.reshape(COPIES, OWN_ROWS, LANES), inverse, scales, *flat)
    shape = (tiles, rows, lanes)
    return master_new.reshape(shape), first_new.reshape(shape), second_new.reshape(shape), codes, rollout_scales


def solution(mesh):
    split = P("fsdp", "replica", None)
    return jax.shard_map(
        on_device,
        mesh=mesh,
        in_specs=(split, split, split, split, P()),
        out_specs=(split, split, split, P("fsdp", None, None), P("fsdp")),
        check_vma=False,
    )
```

time: 75.2 us -> 68.3 us (0.908)
  the two profiles are of different devices: /device:TPU:68 before, /device:TPU:66 now
where the time goes in v2:
time: 68.3 us; the launch traced here: 68.1 us
  Pallas kernels  67.5 us (99%)
    pallas_call x1, Pallas kernels, on_device(): pl.pallas_call(exchange, out_shape=(jax.ShapeDtypeStruct((COPIES * OWN_RO...  62.3 us
    pallas_call x1, Pallas kernels, on_device(): pl.pallas_call(finish, out_shape=(jax.ShapeDtypeStruct((CAP_OWN, 128, 128...  5.22 us

profile of v2, /device:TPU:66, one launch (start us, length us, event | category | flops | bytes accessed | tf_op | source)
XLA Modules:
  0.0 68.1 jit_solution(6734399815947549701)
XLA Ops:
  0.6 62.3 %exchange.1 = (bf16[10752,128]{1,0:T(8,128)(2,1)}, f32[88,128]{1,0:T(8,128)}, f32[8,128]{1,0:T(8,128)}) custom-call(s32[32]{0:T(128)} %counts_ref.1, f32[448,128]{1,0:T(8,128)} %bitcast.9, bf16[448,128]{1,0:T(8,128)(2,1)} %bitcast.15, f32[448,128]{1,0:T(8,128)} %bitcast.11, f32[448,128]{1,0:T(8,128)} %bitcast.13), custom_call_target="tpu_custom_call" | custom-call | tf_op jit(solution)/shard_map/exchange/pallas_call | solution.py:394
  62.9 5.2 %finish.1 = (bf16[84,128,128]{2,1,0:T(8,128)(2,1)}, bf16[84]{0:T(256)(128)(2,1)}, f32[448,128]{1,0:T(8,128)}, f32[448,128]{1,0:T(8,128)}, f32[448,128]{1,0:T(8,128)}) custom-call(bf16[16,672,128]{2,1,0:T(8,128)(2,1)} %bitcast.8, f32[88,128]{1,0:T(8,128)} %get-tuple-element.14.inverse_ref, f32[8,128]{1,0:T(8,128)} %get-tuple-element.15.scale_ref, ...), custom_call_target="tpu_custom_call" | custom-call | tf_op jit(solution)/shard_map/finish/pallas_call | solution.py:429

commit v3 on v2

--- a/solution.py
+++ b/solution.py
@@ -29,7 +29,7 @@
 OWN_ROWS = CAP_OWN * ROWS
 PIECES = ((0, 256), (256, 256), (512, 160))
 VMEM_LIMIT = 63 << 20
-GROUP = 16
+GROUP = 14
 REACH = 22
 
 
@@ -44,8 +44,9 @@
 
 def exchange(
     counts_ref, master_in, gradient_in, first_in, second_in,
-    all_ref, inverse_ref, scales_ref,
-    master_ref, gradient_ref, first_ref, second_ref, in_sem, raw, send, recv, own, peak, peak_z, peak_y, table,
+    codes_out, scales_out, master_out, first_out, second_out,
+    master_ref, gradient_ref, first_ref, second_ref, in_sem,
+    all_ref, codes, inverse_ref, scales_ref, out_sem, raw, send, recv, own, peak, peak_z, peak_y, table,
     a2a_send, a2a_recv, peak_send, peak_recv, gather_send, z_near, z_far, y_near, y_far, local_sem,
 ):
     f = lax.axis_index("fsdp")
@@ -92,7 +93,12 @@
     peaks = jnp.zeros((ROWS, LANES), jnp.float32)
     for step in range(CB // 8):
         here = pl.ds(step * span, span)
-        master_new, _, _ = adam(master_ref[here, :], gradient_ref[here, :], first_ref[here, :], second_ref[here, :])
+        master_new, first_new, second_new = adam(
+            master_ref[here, :], gradient_ref[here, :], first_ref[here, :], second_ref[here, :]
+        )
+        master_ref[here, :] = master_new
+        first_ref[here, :] = first_new
+        second_ref[here, :] = second_new
         raw[here, :] = master_new.astype(jnp.bfloat16)
         tall = jnp.max(jnp.abs(master_new).reshape(8, ROWS, LANES), axis=1)
         peaks = jnp.where(lane == row + step * 8, jnp.max(tall, axis=1, keepdims=True), peaks)
@@ -151,6 +157,17 @@
             ).start()
 
         owners(give)
+
+    leaving = []
+
+    def leave(source, target):
+        copy = pltpu.make_async_copy(source, target, out_sem.at[len(leaving)])
+        copy.start()
+        leaving.append(copy)
+
+    leave(master_ref, master_out)
+    leave(first_ref, first_out)
+    leave(second_ref, second_out)
 
     def tell(source, target, send_sem, recv_sem, device):
         copy = pltpu.make_async_remote_copy(
@@ -290,7 +307,32 @@
             filled = slot < count
             inverse_ref[pl.ds(step * 8, 8), :] = jnp.where(filled, 1.0 / scale, 0.0)
             flat = jnp.where((lane == slot) & filled, scale, flat)
-        scales_ref[...] = jnp.broadcast_to(jnp.max(flat, axis=0, keepdims=True), (ROWS, LANES))
+        scales_ref[...] = jnp.max(flat, axis=0)[:CAP_OWN].astype(jnp.bfloat16)
+        leave(scales_ref, scales_out)
+
+    def code(z_step, piece):
+        low, number = PIECES[piece]
+        part = number // 2
+        for way in range(2):
+            landed(chunk(z_at(z_step), y_at(2), low + way * part, part), y_far.at[way, z_step, piece])
+        if z_step == 0:
+            locals_[piece].wait()
+        first_slot, slots = low // ROWS, number // ROWS
+        top = pl.multiple_of(z_at(z_step) * 32, 32)
+        for base in range(first_slot, first_slot + slots, 8):
+            count_here = min(8, first_slot + slots - base)
+            factor = inverse_ref[pl.ds(base, count_here), :][:, None, :]
+            for pair in range(2):
+                parts = []
+                for k in range(2):
+                    place = (z_at(z_step) * 4 + pair * 2 + k) * OWN_ROWS + base * ROWS
+                    tiles = all_ref[pl.ds(pl.multiple_of(place, 16), count_here * ROWS), :]
+                    parts.append(tiles.astype(jnp.float32).reshape(count_here, ROWS, LANES))
+                both = jnp.concatenate(parts, axis=1)
+                coded = jnp.where(factor > 0.0, both * factor, 0.0).astype(jnp.bfloat16)
+                codes[pl.ds(base, count_here), pl.ds(pl.multiple_of(top + pair * 16, 16), 16), :] = coded
+        here = (pl.ds(first_slot, slots), pl.ds(top, 32))
+        leave(codes.at[here], codes_out.at[here])
 
     relay_y(0, 0)
     relay_z(0)
@@ -307,102 +349,74 @@
     relay_y(3, 1)
     finish_z(1)
     scales()
+    code(0, 0)
     relay_y(2, 0)
+    code(0, 1)
+    code(0, 2)
     finish_z(2)
     relay_y(1, 2)
     relay_y(3, 2)
+    code(3, 0)
+    code(1, 0)
     relay_y(2, 1)
+    code(3, 1)
+    code(1, 1)
     relay_y(2, 2)
-    for piece, (low, number) in enumerate(PIECES):
-        part = number // 2
-        for z_step in range(4):
-            for way in range(2):
-                landed(chunk(z_at(z_step), y_at(2), low + way * part, part), y_far.at[way, z_step, piece])
-    for keep in locals_:
-        keep.wait()
+    code(2, 0)
+    code(3, 2)
+    code(1, 2)
+    code(2, 1)
+    code(2, 2)
     landed(send.at[pl.ds(0, (REACH - 1) * 48)], a2a_send)
     landed(all_ref.at[pl.ds(0, 15 * OWN_ROWS)], gather_send)
+    for copy in leaving:
+        copy.wait()
 
 
 def finish(
-    all_ref, inverse_ref, scale_ref, master_ref, gradient_ref, first_ref, second_ref,
-    codes_ref, scales_ref, master_out, first_out, second_out,
-    tiles, codes, inverse, master, gradient, first, second, master_to, first_to, second_to,
-    tile_sem, small_sem, out_sem,
+    codes_ref, scales_ref, master_ref, first_ref, second_ref,
+    codes_out, scales_out, master_out, first_out, second_out,
+    codes, scales, master, first, second, in_sem, out_sem,
 ):
-    def started(source, target, sem):
-        copy = pltpu.make_async_copy(source, target, sem)
+    ways = [(codes_ref.at[pl.ds(low, GROUP)], codes.at[pl.ds(low, GROUP)], codes_out.at[pl.ds(low, GROUP)]) for low in range(0, CAP_OWN, GROUP)]
+    ways += [(master_ref, master, master_out), (first_ref, first, first_out), (second_ref, second, second_out)]
+    ways += [(scales_ref, scales, scales_out)]
+    into = [pltpu.make_async_copy(source, here, in_sem.at[i]) for i, (source, here, _) in enumerate(ways)]
+    out = [pltpu.make_async_copy(here, target, out_sem.at[i]) for i, (_, here, target) in enumerate(ways)]
+    for copy in into:
         copy.start()
-        return copy
-
-    small = [
-        started(source, target, small_sem.at[i])
-        for i, (source, target) in enumerate(
-            ((master_ref, master), (gradient_ref, gradient), (first_ref, first), (second_ref, second), (inverse_ref, inverse))
-        )
-    ]
-    steps = [(low, min(GROUP, CAP_OWN - low)) for low in range(0, CAP_OWN, GROUP)]
-    arriving = []
-    for i, (low, slots) in enumerate(steps):
-        rows = pl.ds(low * ROWS, slots * ROWS)
-        arriving.append(started(all_ref.at[:, rows, :], tiles.at[:, rows, :], tile_sem.at[i]))
-    for copy in small:
-        copy.wait()
-    leaving = []
-    span = 8 * ROWS
-
-    def update(step, carry):
-        here = pl.ds(pl.multiple_of(step * span, span), span)
-        master_new, first_new, second_new = adam(master[here, :], gradient[here, :], first[here, :], second[here, :])
-        master_to[here, :] = master_new
-        first_to[here, :] = first_new
-        second_to[here, :] = second_new
-        return carry
-
-    lax.fori_loop(0, CB // 8, update, 0)
-    for i, (source, target) in enumerate(((master_to, master_out), (first_to, first_out), (second_to, second_out))):
-        leaving.append(started(source, target, out_sem.at[i]))
-    for i, (low, slots) in enumerate(steps):
-        arriving[i].wait()
-        for base in range(low, low + slots, 8):
-            number = min(8, CAP_OWN - base)
-            factor = inverse[pl.ds(base, number), :][:, None, :]
-            for pair in range(COPIES // 2):
-                parts = [
-                    tiles[2 * pair + k, pl.ds(base * ROWS, number * ROWS), :].astype(jnp.float32).reshape(number, ROWS, LANES)
-                    for k in range(2)
-                ]
-                both = jnp.concatenate(parts, axis=1)
-                coded = jnp.where(factor > 0.0, both * factor, 0.0).astype(jnp.bfloat16)
-                codes[pl.ds(base, number), pl.ds(pair * 16, 16), :] = coded
-        here = pl.ds(low, slots)
-        leaving.append(started(codes.at[here], codes_ref.at[here], out_sem.at[3 + i]))
-    scales_ref[...] = scale_ref[0, :][:CAP_OWN].astype(jnp.bfloat16)
-    for copy in leaving:
+    for arriving, leaving in zip(into, out):
+        arriving.wait()
+        leaving.start()
+    for copy in out:
         copy.wait()
 
 
 def on_device(master, gradient, first_moment, second_moment, owner_counts):
     tiles, rows, lanes = master.shape
     flat = [a.reshape(tiles * rows, lanes) for a in (master, gradient, first_moment, second_moment)]
-    vmem = pl.BlockSpec(memory_space=pltpu.VMEM)
     hbm = pl.BlockSpec(memory_space=pl.ANY)
     dma = pltpu.SemaphoreType.DMA
     part = jax.ShapeDtypeStruct((tiles * rows, lanes), jnp.float32)
-    tile = jax.ShapeDtypeStruct((ROWS, LANES), jnp.float32)
     own = pltpu.VMEM((tiles * rows, lanes), jnp.float32)
-    gathered, inverse, scales = pl.pallas_call(
+    results = (
+        jax.ShapeDtypeStruct((CAP_OWN, 128, 128), jnp.bfloat16),
+        jax.ShapeDtypeStruct((CAP_OWN,), jnp.bfloat16),
+        part, part, part,
+    )
+    found = pl.pallas_call(
         exchange,
-        out_shape=(
-            jax.ShapeDtypeStruct((COPIES * OWN_ROWS, LANES), jnp.bfloat16),
-            jax.ShapeDtypeStruct((88, LANES), jnp.float32),
-            tile,
-        ),
+        out_shape=results,
         in_specs=[pl.BlockSpec(memory_space=pltpu.SMEM)] + [hbm] * 4,
-        out_specs=(vmem, vmem, vmem),
+        out_specs=(hbm,) * 5,
         scratch_shapes=[
             own, pltpu.VMEM((tiles * rows, lanes), jnp.bfloat16), own, own,
             dma((4,)),
+            pltpu.VMEM((COPIES * OWN_ROWS, LANES), jnp.bfloat16),
+            pltpu.VMEM((CAP_OWN, 128, 128), jnp.bfloat16),
+            pltpu.VMEM((88, LANES), jnp.float32),
+            pltpu.VMEM((CAP_OWN,), jnp.bfloat16),
+            dma((16,)),
             pltpu.VMEM((CB * ROWS, LANES), jnp.bfloat16),
             pltpu.VMEM((REACH * 48, LANES), jnp.bfloat16),
             pltpu.VMEM((3 * 512, LANES), jnp.bfloat16),
@@ -425,28 +439,21 @@
         compiler_params=pltpu.CompilerParams(collective_id=0, has_side_effects=True, vmem_limit_bytes=VMEM_LIMIT),
         name="exchange",
     )(owner_counts, *flat)
-    steps = -(-CAP_OWN // GROUP)
     codes, rollout_scales, master_new, first_new, second_new = pl.pallas_call(
         finish,
-        out_shape=(
-            jax.ShapeDtypeStruct((CAP_OWN, 128, 128), jnp.bfloat16),
-            jax.ShapeDtypeStruct((CAP_OWN,), jnp.bfloat16),
-            part, part, part,
-        ),
-        in_specs=[hbm, hbm, vmem] + [hbm] * 4,
-        out_specs=(hbm, vmem, hbm, hbm, hbm),
+        out_shape=results,
+        in_specs=[hbm] * 5,
+        out_specs=(hbm,) * 5,
         scratch_shapes=[
-            pltpu.VMEM((COPIES, OWN_ROWS, LANES), jnp.bfloat16),
             pltpu.VMEM((CAP_OWN, 128, 128), jnp.bfloat16),
-            pltpu.VMEM((88, LANES), jnp.float32),
-            own, pltpu.VMEM((tiles * rows, lanes), jnp.bfloat16), own, own, own, own, own,
-            dma((steps,)),
-            dma((5,)),
-            dma((3 + steps,)),
+            pltpu.VMEM((CAP_OWN,), jnp.bfloat16),
+            own, own, own,
+            dma((CAP_OWN // GROUP + 4,)),
+            dma((CAP_OWN // GROUP + 4,)),
         ],
         compiler_params=pltpu.CompilerParams(vmem_limit_bytes=VMEM_LIMIT),
         name="finish",
-    )(gathered.reshape(COPIES, OWN_ROWS, LANES), inverse, scales, *flat)
+    )(*found)
     shape = (tiles, rows, lanes)
     return master_new.reshape(shape), first_new.reshape(shape), second_new.reshape(shape), codes, rollout_scales
 

time: 68.3 us -> 65.3 us (0.956)
  Pallas kernels: 67.5 us -> 64.5 us
    pallas_call x2, Pallas kernels: 67.5 us -> 64.5 us  [the longest x1 61.6 us: on_device(): pl.pallas_call(exchange, out_shape=results, in_specs=[pl.BlockSpec(memory...]
where the time goes in v3:
time: 65.3 us; the launch traced here: 65.2 us
  Pallas kernels  64.5 us (99%)
    pallas_call x1, Pallas kernels, on_device(): pl.pallas_call(exchange, out_shape=results, in_specs=[pl.BlockSpec(memory...  61.6 us
    pallas_call x1, Pallas kernels, on_device(): pl.pallas_call(finish, out_shape=results, in_specs=[hbm] * 5, out_specs=(...  2.94 us

profile of v3, /device:TPU:66, one launch (start us, length us, event | category | flops | bytes accessed | tf_op | source)
XLA Modules:
  0.0 65.2 jit_solution(10479425349367462162)
XLA Ops:
  0.6 61.6 %exchange.1 = (bf16[84,128,128]{2,1,0:T(8,128)(2,1)}, bf16[84]{0:T(256)(128)(2,1)}, f32[448,128]{1,0:T(8,128)}, f32[448,128]{1,0:T(8,128)}, f32[448,128]{1,0:T(8,128)}) custom-call(s32[32]{0:T(128)} %counts_ref.1, f32[448,128]{1,0:T(8,128)} %bitcast.7, bf16[448,128]{1,0:T(8,128)(2,1)} %bitcast.10, f32[448,128]{1,0:T(8,128)} %bitcast.8, f32[448,128]{1,0:T(8,128)} %bitcast.9), custom_call_target="tpu_custom_call" | custom-call | tf_op jit(solution)/shard_map/exchange/pallas_call | solution.py:407
  62.2 2.9 %finish.1 = (bf16[84,128,128]{2,1,0:T(8,128)(2,1)}, bf16[84]{0:T(256)(128)(2,1)}, f32[448,128]{1,0:T(8,128)}, f32[448,128]{1,0:T(8,128)}, f32[448,128]{1,0:T(8,128)}) custom-call(bf16[84,128,128]{2,1,0:T(8,128)(2,1)} %get-tuple-element.15.codes_ref, bf16[84]{0:T(256)(128)(2,1)} %get-tuple-element.16.scales_ref, f32[448,128]{1,0:T(8,128)} %get-tuple-element.17.master_ref, ...), custom_call_target="tpu_custom_call" | custom-call | tf_op jit(solution)/shard_map/finish/pallas_call | solution.py:442

commit v4 on v3

--- a/solution.py
+++ b/solution.py
@@ -27,10 +27,15 @@
 LANES = 128
 PER_PAIR = 6
 OWN_ROWS = CAP_OWN * ROWS
-PIECES = ((0, 256), (256, 256), (512, 160))
+ARRIVED = (32, 64, 84)
+DIRECT = ()
+PIECES = ((0, 32), (32, 192), (224, 448))
 VMEM_LIMIT = 63 << 20
 GROUP = 14
 REACH = 22
+
+
+ORDER = 'ry00 rz0 py ry01 rz1 ry02 pf ry10 ry30 fz0 rz2 ry11 ry31 fz1 sc co00 ry20 co01 co02 fz2 ry12 ry32 co30 co10 ry21 co31 co11 ry22 co20 co32 co12 co21 co22'
 
 
 def adam(master, gradient, first_moment, second_moment):
@@ -206,7 +211,7 @@
             tiles = halves[half]
             for bit in range(4):
                 tiles = [jnp.where(odd[bit], tiles[(k + (1 << bit)) % RB], tiles[k]) for k in range(RB)]
-            slots = min(RB, PIECES[piece][1] // ROWS - half * RB)
+            slots = min(RB, ARRIVED[piece] - piece * 32 - half * RB)
             for k in range(0, slots, 2):
                 both = jnp.concatenate([tiles[k], tiles[k + 1]], axis=0).astype(jnp.bfloat16)
                 own[pl.ds((piece * 32 + half * 16 + k) * ROWS, 16), :] = both
@@ -227,18 +232,22 @@
         source = own.at[pl.ds(low, number)] if z_step == 0 else place
         for way, step in enumerate((1, -1)):
             tell(source, place, gather_send, y_near.at[way, z_step, piece], at_y(step))
+        if (z_step, piece) in DIRECT:
+            tell(source, place, gather_send, y_far.at[0, z_step, piece], at_y(2))
 
     locals_ = []
-    for piece, (low, number) in enumerate(PIECES):
-        landed_from_all(recv, piece * 512, 16, a2a_recv.at[piece])
-        order(piece)
-        here = own.at[pl.ds(low, number)]
-        for way, step in enumerate((1, -1)):
-            tell(here, chunk(zh, y, low, number), gather_send, z_near.at[way, piece], at_z(step))
-        send_y(0, piece)
-        keep = pltpu.make_async_copy(here, chunk(zh, y, low, number), local_sem.at[piece])
-        keep.start()
-        locals_.append(keep)
+    for part in range(3):
+        landed_from_all(recv, part * 512, 16, a2a_recv.at[part])
+        order(part)
+        for piece, (low, number) in enumerate(PIECES):
+            if piece == len(locals_) and low + number <= ARRIVED[part] * ROWS:
+                here = own.at[pl.ds(low, number)]
+                for way, step in enumerate((1, -1)):
+                    tell(here, chunk(zh, y, low, number), gather_send, z_near.at[way, piece], at_z(step))
+                send_y(0, piece)
+                keep = pltpu.make_async_copy(here, chunk(zh, y, low, number), local_sem.at[piece])
+                keep.start()
+                locals_.append(keep)
 
     def relay_z(piece):
         low, number = PIECES[piece]
@@ -261,6 +270,8 @@
         part = number // 2
         for way, step in enumerate((1, -1)):
             landed(chunk(z_at(z_step), y_at(-step), low, number), y_near.at[way, z_step, piece])
+            if (z_step, piece) in DIRECT:
+                continue
             half = chunk(z_at(z_step), y_at(-step), low + way * part, part)
             tell(half, half, gather_send, y_far.at[way, z_step, piece], at_y(step))
 
@@ -313,8 +324,11 @@
     def code(z_step, piece):
         low, number = PIECES[piece]
         part = number // 2
-        for way in range(2):
-            landed(chunk(z_at(z_step), y_at(2), low + way * part, part), y_far.at[way, z_step, piece])
+        if (z_step, piece) in DIRECT:
+            landed(chunk(z_at(z_step), y_at(2), low, number), y_far.at[0, z_step, piece])
+        else:
+            for way in range(2):
+                landed(chunk(z_at(z_step), y_at(2), low + way * part, part), y_far.at[way, z_step, piece])
         if z_step == 0:
             locals_[piece].wait()
         first_slot, slots = low // ROWS, number // ROWS
@@ -334,39 +348,11 @@
         here = (pl.ds(first_slot, slots), pl.ds(top, 32))
         leave(codes.at[here], codes_out.at[here])
 
-    relay_y(0, 0)
-    relay_z(0)
-    peaks_y()
-    relay_y(0, 1)
-    relay_z(1)
-    relay_y(0, 2)
-    peaks_f()
-    relay_y(1, 0)
-    relay_y(3, 0)
-    finish_z(0)
-    relay_z(2)
-    relay_y(1, 1)
-    relay_y(3, 1)
-    finish_z(1)
-    scales()
-    code(0, 0)
-    relay_y(2, 0)
-    code(0, 1)
-    code(0, 2)
-    finish_z(2)
-    relay_y(1, 2)
-    relay_y(3, 2)
-    code(3, 0)
-    code(1, 0)
-    relay_y(2, 1)
-    code(3, 1)
-    code(1, 1)
-    relay_y(2, 2)
-    code(2, 0)
-    code(3, 2)
-    code(1, 2)
-    code(2, 1)
-    code(2, 2)
+    tasks = dict(
+        ry=relay_y, rz=relay_z, fz=finish_z, co=code, py=peaks_y, pf=peaks_f, sc=scales,
+    )
+    for task in ORDER.split():
+        tasks[task[:2]](*[int(digit) for digit in task[2:]])
     landed(send.at[pl.ds(0, (REACH - 1) * 48)], a2a_send)
     landed(all_ref.at[pl.ds(0, 15 * OWN_ROWS)], gather_send)
     for copy in leaving:
@@ -416,7 +402,7 @@
             pltpu.VMEM((CAP_OWN, 128, 128), jnp.bfloat16),
             pltpu.VMEM((88, LANES), jnp.float32),
             pltpu.VMEM((CAP_OWN,), jnp.bfloat16),
-            dma((16,)),
+            dma((4 + 4 * len(PIECES),)),
             pltpu.VMEM((CB * ROWS, LANES), jnp.bfloat16),
             pltpu.VMEM((REACH * 48, LANES), jnp.bfloat16),
             pltpu.VMEM((3 * 512, LANES), jnp.bfloat16),
@@ -430,11 +416,11 @@
             dma((3,)),
             dma((3,)),
             dma,
-            dma((2, 3)),
-            dma((2, 3)),
-            dma((2, 4, 3)),
-            dma((2, 4, 3)),
-            dma((3,)),
+            dma((2, len(PIECES))),
+            dma((2, len(PIECES))),
+            dma((2, 4, len(PIECES))),
+            dma((2, 4, len(PIECES))),
+            dma((len(PIECES),)),
         ],
         compiler_params=pltpu.CompilerParams(collective_id=0, has_side_effects=True, vmem_limit_bytes=VMEM_LIMIT),
         name="exchange",

time: 65.3 us -> 62.4 us (0.956)
  the two profiles are of different devices: /device:TPU:66 before, /device:TPU:34 now
where the time goes in v4:
time: 62.4 us; the launch traced here: 62.2 us
  Pallas kernels  61.6 us (99%)
  between operations  0.64 us (1%)
    pallas_call x1, Pallas kernels, on_device(): pl.pallas_call(exchange, out_shape=results, in_specs=[pl.BlockSpec(memory...  58.7 us
    pallas_call x1, Pallas kernels, on_device(): pl.pallas_call(finish, out_shape=results, in_specs=[hbm] * 5, out_specs=(...  2.94 us

profile of v4, /device:TPU:34, one launch (start us, length us, event | category | flops | bytes accessed | tf_op | source)
XLA Modules:
  0.0 62.2 jit_solution(3923988095548464969)
XLA Ops:
  0.6 58.7 %exchange.1 = (bf16[84,128,128]{2,1,0:T(8,128)(2,1)}, bf16[84]{0:T(256)(128)(2,1)}, f32[448,128]{1,0:T(8,128)}, f32[448,128]{1,0:T(8,128)}, f32[448,128]{1,0:T(8,128)}) custom-call(s32[32]{0:T(128)} %counts_ref.1, f32[448,128]{1,0:T(8,128)} %bitcast.7, bf16[448,128]{1,0:T(8,128)(2,1)} %bitcast.10, f32[448,128]{1,0:T(8,128)} %bitcast.8, f32[448,128]{1,0:T(8,128)} %bitcast.9), custom_call_target="tpu_custom_call" | custom-call | tf_op jit(solution)/shard_map/exchange/pallas_call | solution.py:393
  59.3 2.9 %finish.1 = (bf16[84,128,128]{2,1,0:T(8,128)(2,1)}, bf16[84]{0:T(256)(128)(2,1)}, f32[448,128]{1,0:T(8,128)}, f32[448,128]{1,0:T(8,128)}, f32[448,128]{1,0:T(8,128)}) custom-call(bf16[84,128,128]{2,1,0:T(8,128)(2,1)} %get-tuple-element.15.codes_ref, bf16[84]{0:T(256)(128)(2,1)} %get-tuple-element.16.scales_ref, f32[448,128]{1,0:T(8,128)} %get-tuple-element.17.master_ref, ...), custom_call_target="tpu_custom_call" | custom-call | tf_op jit(solution)/shard_map/finish/pallas_call | solution.py:428

commit v5 on v4

--- a/solution.py
+++ b/solution.py
@@ -364,9 +364,11 @@
     codes_out, scales_out, master_out, first_out, second_out,
     codes, scales, master, first, second, in_sem, out_sem,
 ):
-    ways = [(codes_ref.at[pl.ds(low, GROUP)], codes.at[pl.ds(low, GROUP)], codes_out.at[pl.ds(low, GROUP)]) for low in range(0, CAP_OWN, GROUP)]
+    ways = [(scales_ref, scales, scales_out)]
     ways += [(master_ref, master, master_out), (first_ref, first, first_out), (second_ref, second, second_out)]
-    ways += [(scales_ref, scales, scales_out)]
+    for low in range(0, CAP_OWN, GROUP):
+        part = pl.ds(low, GROUP)
+        ways.append((codes_ref.at[part], codes.at[part], codes_out.at[part]))
     into = [pltpu.make_async_copy(source, here, in_sem.at[i]) for i, (source, here, _) in enumerate(ways)]
     out = [pltpu.make_async_copy(here, target, out_sem.at[i]) for i, (_, here, target) in enumerate(ways)]
     for copy in into:

time: 62.4 us -> 62.8 us (level)
  no operation moved by 1% of the time
where the time goes in v5:
time: 62.8 us; the launch traced here: 62.6 us
  Pallas kernels  62 us (99%)
  between operations  0.64 us (1%)
    pallas_call x1, Pallas kernels, on_device(): pl.pallas_call(exchange, out_shape=results, in_specs=[pl.BlockSpec(memory...  58.7 us
    pallas_call x1, Pallas kernels, on_device(): pl.pallas_call(finish, out_shape=results, in_specs=[hbm] * 5, out_specs=(...  3.32 us

profile of v5, /device:TPU:34, one launch (start us, length us, event | category | flops | bytes accessed | tf_op | source)
XLA Modules:
  0.0 62.6 jit_solution(11236837328992669014)
XLA Ops:
  0.6 58.7 %exchange.1 = (bf16[84,128,128]{2,1,0:T(8,128)(2,1)}, bf16[84]{0:T(256)(128)(2,1)}, f32[448,128]{1,0:T(8,128)}, f32[448,128]{1,0:T(8,128)}, f32[448,128]{1,0:T(8,128)}) custom-call(s32[32]{0:T(128)} %counts_ref.1, f32[448,128]{1,0:T(8,128)} %bitcast.7, bf16[448,128]{1,0:T(8,128)(2,1)} %bitcast.10, f32[448,128]{1,0:T(8,128)} %bitcast.8, f32[448,128]{1,0:T(8,128)} %bitcast.9), custom_call_target="tpu_custom_call" | custom-call | tf_op jit(solution)/shard_map/exchange/pallas_call | solution.py:395
  59.3 3.3 %finish.1 = (bf16[84,128,128]{2,1,0:T(8,128)(2,1)}, bf16[84]{0:T(256)(128)(2,1)}, f32[448,128]{1,0:T(8,128)}, f32[448,128]{1,0:T(8,128)}, f32[448,128]{1,0:T(8,128)}) custom-call(bf16[84,128,128]{2,1,0:T(8,128)(2,1)} %get-tuple-element.15.codes_ref, bf16[84]{0:T(256)(128)(2,1)} %get-tuple-element.16.scales_ref, f32[448,128]{1,0:T(8,128)} %get-tuple-element.17.master_ref, ...), custom_call_target="tpu_custom_call" | custom-call | tf_op jit(solution)/shard_map/finish/pallas_call | solution.py:430
